TPU v7x, 32 devices: a whole 2x2x4 slice. The times are simulated.
32 devices in a mesh: owner: 8 (over y, x, core), split: 4 (over z).
Axes of the slice: x: 2, y: 2, z: 4, core: 2. Of those that a mesh axis runs over, the one named last changes fastest.
Arguments:
- embeddings: bfloat16 [32768, 1024], P(('owner', 'split')), may hold values from -6 to 6
- row_dest: int32 [32768, 1], P(('owner', 'split')), may hold values from 0 to 39; in each aligned block of 1024 rows (0 to 1023, 1024 to 2047, ...) at most 51 rows name the same one
- row_cluster: int32 [32768], P(('owner', 'split')), may hold values from 0 to 7
Outputs:
- best_similarity: float32 [32768], P(('owner', 'split'))
Inputs may be any that keep to these rules, and one draw needn't show every extreme that they name: `row_dest`: among the rows of one source shard no destination is named more than 51 times, a bound that some block reaches.
All inputs are finite; a program needn't handle non-finite values.
Results may differ from a plain program's by a relative error of at most 0.0016.
Values may be sent and summed in bfloat16 or wider, within the bound.
A program may use at most 64 MiB of HBM per device.

v0:
```python
import jax
import jax.numpy as jnp
from jax import lax
from jax.sharding import PartitionSpec as P


def unit_rows(embeddings):
    values = embeddings.astype(jnp.float32)
    scale = lax.rsqrt(jnp.sum(values * values, axis=1, keepdims=True) + 1e-06)
    return (values * scale).astype(jnp.bfloat16)


def pair_scores(left_rows, right_rows):
    return lax.dot_general(
        left_rows, right_rows, (((1,), (1,)), ((), ())), preferred_element_type=jnp.float32
    )


def on_device(embeddings, row_dest, row_cluster):
    n_owner = lax.axis_size("owner")
    n_split = lax.axis_size("split")
    devices = n_owner * n_split
    ndest = devices + n_owner
    shard_rows = embeddings.shape[0]
    width = embeddings.shape[1]
    capacity = max(2, 2 * shard_rows // ndest)
    unit = unit_rows(embeddings)
    destinations = row_dest[:, 0]
    targets = jnp.arange(ndest, dtype=jnp.int32)
    onehot = (destinations[:, None] == targets[None, :]).astype(jnp.int32)
    slots = jnp.sum(onehot * (jnp.cumsum(onehot, axis=0) - 1), axis=1)
    table = (
        jnp.full((ndest, capacity), -1, jnp.int32)
        .at[destinations, slots]
        .set(jnp.arange(shard_rows, dtype=jnp.int32))
    )
    valid = table >= 0
    safe_ids = jnp.maximum(table, 0)
    is_giant = targets >= devices
    send_keys = jnp.where(valid, jnp.where(is_giant[:, None], 0, row_cluster[safe_ids]), -1)
    send_rows = jnp.where(valid[:, :, None], unit[safe_ids], jnp.zeros((), jnp.bfloat16))
    local_rows = send_rows[:devices]
    local_keys = send_keys[:devices]
    moved_rows, moved_keys = (
        lax.all_to_all(local_rows, ("owner", "split"), split_axis=0, concat_axis=0, tiled=True),
        lax.all_to_all(local_keys, ("owner", "split"), split_axis=0, concat_axis=0, tiled=True),
    )
    giant_rows, giant_keys = (
        lax.all_to_all(send_rows[devices:], "owner", split_axis=0, concat_axis=0, tiled=True),
        lax.all_to_all(send_keys[devices:], "owner", split_axis=0, concat_axis=0, tiled=True),
    )
    flat_rows = moved_rows.reshape(devices * capacity, width)
    flat_keys = moved_keys.reshape(devices * capacity)
    total_rows = devices * capacity
    sources_per = 1
    while sources_per < devices and sources_per * capacity < 512:
        sources_per = sources_per * 2
    block_rows = sources_per * capacity
    column_index = jnp.arange(total_rows, dtype=jnp.int32)

    def block_best(block_number):
        first = block_number * block_rows
        query_rows = lax.dynamic_slice_in_dim(flat_rows, first, block_rows, 0)
        query_keys = lax.dynamic_slice_in_dim(flat_keys, first, block_rows, 0)
        row_index = first + jnp.arange(block_rows, dtype=jnp.int32)
        scores = pair_scores(query_rows, flat_rows)
        mask = (query_keys[:, None] == flat_keys[None, :]) & (query_keys[:, None] >= 0)
        mask = mask & (row_index[:, None] != column_index[None, :])
        return jnp.max(jnp.where(mask, scores, jnp.float32(-1.0)), axis=1)

    local_best = lax.map(block_best, jnp.arange(total_rows // block_rows, dtype=jnp.int32)).reshape(
        devices, capacity
    )
    own_rows = giant_rows.reshape(n_owner * capacity, width)
    own_keys = giant_keys.reshape(n_owner * capacity)
    own_count = n_owner * capacity
    own_index = lax.axis_index("split") * own_count + jnp.arange(own_count, dtype=jnp.int32)
    start_value = jnp.full((own_count,), -1.0, jnp.float32)
    piece_rows = lax.all_gather(giant_rows, "split", axis=0, tiled=True)
    piece_keys = lax.all_gather(giant_keys, "split", axis=0, tiled=True)
    other_rows = piece_rows.reshape(-1, width)
    other_keys = piece_keys.reshape(-1)
    other_index = jnp.arange(other_keys.shape[0], dtype=jnp.int32)
    scores = pair_scores(own_rows, other_rows)
    mask = (own_keys[:, None] >= 0) & (other_keys[None, :] >= 0)
    mask = mask & (own_index[:, None] != other_index[None, :])
    giant_best = jnp.maximum(
        start_value, jnp.max(jnp.where(mask, scores, jnp.float32(-1.0)), axis=1)
    )
    local_back = lax.all_to_all(
        local_best, ("owner", "split"), split_axis=0, concat_axis=0, tiled=True
    )
    giant_back = lax.all_to_all(
        giant_best.reshape(n_owner, capacity), "owner", split_axis=0, concat_axis=0, tiled=True
    )
    results = jnp.concatenate([local_back, giant_back], axis=0)
    return results[destinations, slots]


def solution(mesh):
    placed = (P(("owner", "split"), None), P(("owner", "split"), None), P(("owner", "split")))
    return jax.shard_map(
        on_device, mesh=mesh, in_specs=placed, out_specs=P(("owner", "split")), check_vma=False
    )
```

profile of v0, /device:TPU:0, one launch (start us, length us, event | category | flops | bytes accessed | tf_op | source)
XLA Modules:
  0.0 299.3 jit_solution(3786032942848659343)
XLA Ops:
  6.5 0.7 fusion.11
  7.3 11.3 %reduce-window.6 = s32[40,8,128]{2,1,0:T(8,128)S(1)} reduce-window(s32[40,8,128]{2,1,0:T(8,128)S(1)} %fusion.11, s32[]{:T(128)} %constant.26.clone.1), window={size=1x1x128 pad=0_0x0_0x127_0}, to_apply=%region_0.0 | reduce-window | flops 5201920 | bytes 327684 | tf_op jit(solution)/shard_map/reduce-window
  18.5 0.1 slice.30
  18.6 0.1 copy.16
  18.8 0.1 copy.17
  18.9 0.1 add_add_fusion
  19.0 0.7 fusion.10
  19.7 0.7 shift-left_or_fusion
  20.4 0.8 and_reduce_fusion
  21.2 0.7 multiply_reduce_fusion
  22.0 4.3 %scatter_custom_fusion = s32[2040]{0:T(1024)S(1)} fusion(s32[1024]{0:T(1024)S(1)} %broadcast_select_fusion.1, s32[1024]{0:T(1024)S(1)} %iota.36, s32[]{:T(128)} %constant.28.clone.1), kind=kCustom, calls=%fused_computation.41 | custom fusion | bytes 8164
  26.3 0.1 reshape.123
  26.5 0.0 copy-start.2
  26.5 8.6 %gather_fusion = s32[2040]{0:T(1024)S(1)} fusion(s32[1024]{0:T(1024)S(1)} %copy-done, s32[2048]{0:T(1024)S(1)} %pad_clamp_fusion), kind=kCustom, calls=%fused_computation | custom fusion | bytes 24480 | tf_op jit(solution)/shard_map/gather | solution.py:40
  35.1 0.1 reshape.128
  35.2 0.1 select_select_fusion
  35.2 0.6 slice.34
  35.8 5.2 %all-to-all-start.3 = ((s32[8,1,51]{2,1,0:T(1,128)}), s32[8,1,51]{2,1,0:T(1,128)S(1)}, u32[]{:S(2)}, u32[]{:S(2)}) async-start(s32[8,1,51]{2,1,0:T(1,128)} %bitcast.9), calls=%async_computation.3 | async-start | bytes 8192 | tf_op jit(solution)/shard_map/all_to_all | solution.py:50
  41.0 0.0 copy-start.3
  41.0 0.5 fusion.5
  41.5 1.1 copy-done.3
  42.6 0.4 fusion.6
  43.0 0.6 slice.32
  43.6 9.7 %gather_fusion.1 = bf16[2040,1024]{1,0:T(8,128)(2,1)} fusion(bf16[1024,1024]{1,0:T(8,128)(2,1)S(1)} %fusion.6, s32[2048]{0:T(1024)S(1)} %pad_clamp_fusion), kind=kCustom, calls=%fused_computation.1 | custom fusion | bytes 8364000 | tf_op jit(solution)/shard_map/gather | solution.py:41
  53.3 6.4 %reshape.136 = bf16[40,51,1024]{2,1,0:T(8,128)(2,1)} reshape(bf16[2040,1024]{1,0:T(8,128)(2,1)} %gather_fusion.1) | data formatting | bytes 8355840 | tf_op jit(solution)/shard_map/gather | solution.py:41
  59.7 0.0 all-to-all-done.3
  59.7 6.3 %all-to-all-start = ((s32[32,1,51]{2,1,0:T(1,128)}), s32[32,1,51]{2,1,0:T(1,128)S(1)}, u32[]{:S(2)}, u32[]{:S(2)}) async-start(s32[32,1,51]{2,1,0:T(1,128)} %bitcast.5), calls=%async_computation | async-start | bytes 32768 | tf_op jit(solution)/shard_map/all_to_all | solution.py:46
  66.0 2.6 broadcast_select_fusion
  68.6 2.1 copy-done.1
  70.7 1.0 slice.35
  71.7 1.4 all-to-all-done
  73.2 3.6 %all-to-all-start.4 = ((bf16[8,51,1024]{2,1,0:T(8,128)(2,1)}), bf16[8,51,1024]{2,1,0:T(8,128)(2,1)S(1)}, u32[]{:S(2)}, u32[]{:S(2)}) async-start(bf16[8,51,1024]{2,1,0:T(8,128)(2,1)} %slice.35), calls=%async_computation.4 | async-start | bytes 1835008 | tf_op jit(solution)/shard_map/all_to_all | solution.py:49
  76.7 4.2 %slice.33 = bf16[32,51,1024]{2,1,0:T(8,128)(2,1)} slice(bf16[40,51,1024]{2,1,0:T(8,128)(2,1)} %copy-done.1), slice={[0:32], [0:51], [0:1024]} | slice | bytes 6684672 | tf_op jit(solution)/shard_map/slice | solution.py:42
  81.0 9.7 %all-to-all-done.4 = bf16[8,51,1024]{2,1,0:T(8,128)(2,1)S(1)} async-done(((bf16[8,51,1024]{2,1,0:T(8,128)(2,1)}), bf16[8,51,1024]{2,1,0:T(8,128)(2,1)S(1)}, u32[]{:S(2)}, u32[]{:S(2)}) %all-to-all-start.4) | async-done | bytes 835616 | tf_op jit(solution)/shard_map/all_to_all | solution.py:49
  90.7 3.5 %all-to-all-start.1 = ((bf16[32,51,1024]{2,1,0:T(8,128)(2,1)}), bf16[32,51,1024]{2,1,0:T(8,128)(2,1)}, u32[]{:S(2)}, u32[]{:S(2)}) async-start(bf16[32,51,1024]{2,1,0:T(8,128)(2,1)} %slice.33), calls=%async_computation.1 | async-start | bytes 7340032 | tf_op jit(solution)/shard_map/all_to_all | solution.py:45
  94.2 0.0 all-gather.3.cloned.1.call-start
  94.3 1.4 copy.19
  95.6 0.0 all-gather.3.cloned.1.call-update
  95.7 0.1 ge.50
  95.8 140.3 %all-gather = s32[32,1,51]{2,1,0:T(1,128)S(1)} all-gather(s32[8,1,51]{2,1,0:T(1,128)S(1)} %all-to-all-done.3), channel_id=2, replica_groups=mesh['owner'=8,'split'=4] {'split'}, dimensions={0}, use_global_device_ids=true | all-gather | bytes 8160 | tf_op jit(solution)/shard_map/all_gather | solution.py:80
  236.1 0.1 compare_reduce_fusion
  236.2 0.1 ge.53
  236.3 0.1 eq.69
  236.4 0.5 broadcast.175
  236.9 0.7 reduce.11
  237.6 0.1 reshape.114
  237.7 1.2 reshape.116
  238.9 5.7 %copy.20 = bf16[32,51,1024]{2,1,0:T(8,128)(2,1)} copy(bf16[32,51,1024]{2,0,1:T(8,128)(2,1)} %all-gather.3.cloned.1.call-done) | data formatting | bytes 6684672 | tf_op jit(solution)/shard_map/all_gather | solution.py:79
  244.6 3.3 %reshape.117 = bf16[1632,1024]{1,0:T(8,128)(2,1)S(1)} reshape(bf16[32,51,1024]{2,1,0:T(8,128)(2,1)} %copy.20) | data formatting | bytes 6684672 | tf_op jit(solution)/shard_map/reshape | solution.py:81
  247.8 3.2 %fusion.8 = f32[408]{0:T(512)S(1)} fusion(bf16[408,1024]{1,0:T(8,128)(2,1)} %reshape.116, bf16[1632,1024]{1,0:T(8,128)(2,1)S(1)} %reshape.117, s32[408]{0:T(512)S(1)} %iota_add_fusion.1, pred[1632]{0:T(1024)(128)(4,1)S(1)} %ge.53, pred[408]{0:T(512)(128)(4,1)S(1)} %ge.50), kind=kOutput, calls=%fused_computation.20 | convolution fusion | flops 1367001984 | bytes 4183224 | tf_op jit(solution)/shard_map/dot_general | solution.py:14
  251.0 0.7 max_broadcast_in_dim.15
  251.7 0.0 all-to-all-done.1
  251.7 3.5 %all-to-all-start.5 = ((f32[8,1,51]{2,1,0:T(1,128)}), f32[8,1,51]{2,1,0:T(1,128)S(1)}, u32[]{:S(2)}, u32[]{:S(2)}) async-start(f32[8,1,51]{2,1,0:T(1,128)} %max_broadcast_in_dim.15), calls=%async_computation.5 | async-start | bytes 8192 | tf_op jit(solution)/shard_map/all_to_all | solution.py:93
  255.2 3.3 %reshape.115 = bf16[1632,1024]{1,0:T(8,128)(2,1)S(1)} reshape(bf16[32,51,1024]{2,1,0:T(8,128)(2,1)} %all-to-all-done.1) | data formatting | bytes 6684672 | tf_op jit(solution)/shard_map/reshape | solution.py:52
  258.5 10.6 %while.12 = (s32[]{:T(128)}, f32[2,816]{1,0:T(2,128)S(1)}, s32[2]{0:T(128)S(1)}, s32[1632]{0:T(1024)S(1)}, s32[32,51]{1,0:T(8,128)}, /*index=5*/bf16[1632,1024]{...) while((s32[]{:T(128)}, f32[2,816]{1,0:T(2,128)S(1)}, ...), condition=%wide.wide.region_7.8_spmd.clone, body=%wide.wide.region_5.7_spmd.clone.sunk | while | flops 2735337216 | bytes 5058031 | solution.py:71
  258.5 0.6 dynamic_slice.24
  259.8 0.1 broadcast_compare_fusion.4
  259.9 3.9 %select_reduce_fusion.3 = f32[816]{0:T(1024)S(1)} fusion(bf16[1632,1024]{1,0:T(8,128)(2,1)S(1)} %get-tuple-element.174, s32[816]{0:T(1024)S(1)} %iota_add_fusion.4, s32[1632]{0:T(1024)S(1)} %get-tuple-element.175, s32[816]{0:T(1024)S(1)} %get-tuple-element.145, pred[816]{0:T(1024)(128)(4,1)S(1)} %get-tuple-element.146, s32[]{:T(128)S(6)} %select_n.68), kind=kOutput, calls=%fused_computation.6.clone.clone.1 | convolution fusion | flops 2735335680 | bytes 5034180 | tf_op jit(solution)/shard_map/while/body/eval_jaxpr/dot_general | solution.py:14
  263.8 0.6 dynamic_slice.24
  265.1 0.1 broadcast_compare_fusion.4
  265.1 3.9 %select_reduce_fusion.3 = f32[816]{0:T(1024)S(1)} fusion(bf16[1632,1024]{1,0:T(8,128)(2,1)S(1)} %get-tuple-element.174, s32[816]{0:T(1024)S(1)} %iota_add_fusion.4, s32[1632]{0:T(1024)S(1)} %get-tuple-element.175, s32[816]{0:T(1024)S(1)} %get-tuple-element.145, pred[816]{0:T(1024)(128)(4,1)S(1)} %get-tuple-element.146, s32[]{:T(128)S(6)} %select_n.68), kind=kOutput, calls=%fused_computation.6.clone.clone.1 | convolution fusion | flops 2735335680 | bytes 5034180 | tf_op jit(solution)/shard_map/while/body/eval_jaxpr/dot_general | solution.py:14
  269.1 0.1 all_to_all.40
  269.2 11.8 %all_to_all.55 = f32[32,1,51]{2,1,0:T(1,128)S(1)} all-to-all(f32[32,1,51]{2,1,0:T(1,128)S(1)} %all_to_all.40), channel_id=1, replica_groups=mesh['owner'=8,'split'=4] {'owner','split'}, dimensions={0} | all-to-all | bytes 13056 | tf_op jit(solution)/shard_map/all_to_all | solution.py:90
  281.0 11.5 %gather_fusion.2 = f32[1024]{0:T(1024)} fusion(f32[40,51]{1,0:T(8,128)S(1)} %pad_maximum_fusion, s32[1024]{0:T(1024)S(1)} %bitcast.36), kind=kCustom, calls=%fused_computation.2 | custom fusion | bytes 16384 | tf_op jit(solution)/shard_map/gather | solution.py:97
  (29 shorter events, 0.2 us)
Async XLA Ops:
  6.5 19.9 %copy-start = (s32[1024]{0:T(1024)S(1)}, s32[1024]{0:T(1024)}, u32[]{:S(2)}) copy-start(s32[1024]{0:T(1024)} %param.7) | copy-start | bytes 12292
  26.5 14.6 %copy-start.2 = (bf16[1024,1024]{1,0:T(8,128)(2,1)S(1)}, bf16[1024,1024]{1,0:T(8,128)(2,1)}, u32[]{:S(2)}) copy-start(bf16[1024,1024]{1,0:T(8,128)(2,1)} %param.5) | copy-start | bytes 6291460
  35.8 23.8 %all-to-all-start.3 = ((s32[8,1,51]{2,1,0:T(1,128)}), s32[8,1,51]{2,1,0:T(1,128)S(1)}, u32[]{:S(2)}, u32[]{:S(2)}) async-start(s32[8,1,51]{2,1,0:T(1,128)} %bitcast.9), calls=%async_computation.3 | async-start | bytes 8192 | tf_op jit(solution)/shard_map/all_to_all | solution.py:50
  41.0 1.6 copy-start.3
  59.7 13.5 %all-to-all-start = ((s32[32,1,51]{2,1,0:T(1,128)}), s32[32,1,51]{2,1,0:T(1,128)S(1)}, u32[]{:S(2)}, u32[]{:S(2)}) async-start(s32[32,1,51]{2,1,0:T(1,128)} %bitcast.5), calls=%async_computation | async-start | bytes 32768 | tf_op jit(solution)/shard_map/all_to_all | solution.py:46
  68.6 2.1 copy-start.1
  73.2 163.7 %copy-start.4 = (s32[32,1,51]{2,1,0:T(1,128)}, s32[32,1,51]{2,1,0:T(1,128)S(1)}, u32[]{:S(2)}) copy-start(s32[32,1,51]{2,1,0:T(1,128)S(1)} %all-to-all-done) | copy-start | bytes 19588
  73.2 17.5 %all-to-all-start.4 = ((bf16[8,51,1024]{2,1,0:T(8,128)(2,1)}), bf16[8,51,1024]{2,1,0:T(8,128)(2,1)S(1)}, u32[]{:S(2)}, u32[]{:S(2)}) async-start(bf16[8,51,1024]{2,1,0:T(8,128)(2,1)} %slice.35), calls=%async_computation.4 | async-start | bytes 1835008 | tf_op jit(solution)/shard_map/all_to_all | solution.py:49
  90.7 161.1 %all-to-all-start.1 = ((bf16[32,51,1024]{2,1,0:T(8,128)(2,1)}), bf16[32,51,1024]{2,1,0:T(8,128)(2,1)}, u32[]{:S(2)}, u32[]{:S(2)}) async-start(bf16[32,51,1024]{2,1,0:T(8,128)(2,1)} %slice.33), calls=%async_computation.1 | async-start | bytes 7340032 | tf_op jit(solution)/shard_map/all_to_all | solution.py:45
  94.2 144.6 %all-gather.3.cloned.1.call-start = ((), (), s32[]{:S(2)}) async-start(), calls=%async_computation.6 | async-start | bytes 4177920 | tf_op jit(solution)/shard_map/all_gather | solution.py:79
  251.7 17.5 %all-to-all-start.5 = ((f32[8,1,51]{2,1,0:T(1,128)}), f32[8,1,51]{2,1,0:T(1,128)S(1)}, u32[]{:S(2)}, u32[]{:S(2)}) async-start(f32[8,1,51]{2,1,0:T(1,128)} %max_broadcast_in_dim.15), calls=%async_computation.5 | async-start | bytes 8192 | tf_op jit(solution)/shard_map/all_to_all | solution.py:93
Sparse Core Ops, SparseCore 0:
  96.6 127.6 all-gather.2
where the time goes:
time: 300 us; the launch traced here: 299 us
  blocking collectives  152 us (51%)
  local copies, waits for them, and re-layouts  68.4 us (23%)
  starting transfers between devices  22.1 us (7%)
  other arithmetic  19.6 us (7%)
  between operations  13.7 us (5%)
  waiting for transfers between devices  11.2 us (4%)
  matrix products  10.9 us (4%)
    all_gather x1, blocking collectives, on_device(): piece_keys = lax.all_gather(giant_keys, 'split', axis=0, tiled=True)  140 us
    gather x2, local copies, waits for them, and re-layouts, on_device(): unit[safe_ids]  16.1 us
    all_to_all x1, blocking collectives, on_device(): lax.all_to_all(local_best, ('owner', 'split'), split_axis=0, concat_axis=...  11.8 us
    gather x1, local copies, waits for them, and re-layouts, on_device(): return results[destinations, slots]  11.5 us
    another operation x2, other arithmetic  11.3 us
    dot_general x3, matrix products, pair_scores(): lax.dot_general(left_rows, right_rows, (((1,), (1,)), ((), ())), preferre...  10.9 us
    all_to_all x1, waiting for transfers between devices, on_device(): lax.all_to_all(send_rows[devices:], 'owner', split_axis=0, concat_axis=0,...  9.71 us
    gather x2, local copies, waits for them, and re-layouts, on_device(): row_cluster[safe_ids]  8.69 us
  transfers between devices with their start and end apart: 6, of which 2 were waited for; matrix products, arithmetic and copies ran while one was open for 18% of the time, Pallas kernels for 0%

commit v1 on v0

v1 whole, which is shorter than its diff:
```python
import functools

import jax
import jax.numpy as jnp
from jax import lax
from jax.experimental import pallas as pl
from jax.experimental.pallas import tpu as pltpu
from jax.sharding import PartitionSpec as P

F32 = jnp.float32
BF16 = jnp.bfloat16
MESH = pl.DeviceIdType.MESH


def kernel(
    sizes, emb_ref, dest_ref, cluster_ref, out_ref,
    unit, send, recv, giant, keycol, keyrow, best, resbuf, resrecv,
    send_sem, recv_sem, giant_sem, res_send_sem, res_recv_sem,
):
    n_owner, n_split, cap, rows, per = sizes
    devices = n_owner * n_split
    ndest = devices + n_owner
    shard, width = emb_ref.shape
    chunk = per * rows
    chunks = devices // per
    my_owner = lax.axis_index("owner")
    my_split = lax.axis_index("split")
    me = my_owner * n_split + my_split

    def holder_split(o):
        return n_split // 2 - 1 + lax.rem(o, 2)

    is_holder = my_split == holder_split(my_owner)

    def coords(d):
        return (lax.div(d, n_split), lax.rem(d, n_split))

    def block(number):
        return pl.ds(pl.multiple_of(number * rows, rows), rows)

    barrier = pltpu.get_barrier_semaphore()

    @pl.loop(1, devices)
    def _(i):
        pl.semaphore_signal(barrier, inc=1, device_id=coords(lax.rem(me + i, devices)), device_id_type=MESH)

    strip = 256

    @pl.loop(0, shard // strip)
    def _(i):
        at = pl.ds(pl.multiple_of(i * strip, strip), strip)
        values = emb_ref[at, :].astype(F32)
        scale = lax.rsqrt(jnp.sum(values * values, axis=1, keepdims=True) + 1e-06)
        unit[at, :] = (values * scale).astype(BF16)

    dest = dest_ref[...]
    gpad = (ndest + 15) // 16 * 16
    onehot = (lax.broadcasted_iota(jnp.int32, (gpad, shard), 0) == dest).astype(F32)
    earlier = (
        lax.broadcasted_iota(jnp.int32, (shard, shard), 0) < lax.broadcasted_iota(jnp.int32, (shard, shard), 1)
    ).astype(F32).astype(BF16)
    before = jnp.dot(onehot.astype(BF16), earlier, preferred_element_type=F32)
    slot = jnp.sum(onehot * before, axis=0, keepdims=True).astype(jnp.int32)
    place = dest * rows + slot
    key = jnp.where(dest < devices, cluster_ref[...], 0) + 1
    slot_hot = (lax.broadcasted_iota(jnp.int32, (128, shard), 0) == slot).astype(F32)
    keymat = lax.dot_general(
        (onehot * key.astype(F32)).astype(BF16), slot_hot.astype(BF16), (((1,), (1,)), ((), ())),
        preferred_element_type=F32,
    )
    keyrow[0:gpad, 0:128] = keymat
    resbuf[...] = jnp.zeros_like(resbuf)

    pl.semaphore_wait(barrier, devices - 1)

    def giant_copy(o):
        target = o * n_split + holder_split(o)
        return target, pltpu.make_async_remote_copy(
            src_ref=send.at[block(devices + o)], dst_ref=giant.at[block(me)],
            send_sem=send_sem.at[devices + o], recv_sem=giant_sem.at[me],
            device_id=coords(target), device_id_type=MESH,
        )

    def local_copy(d):
        return pltpu.make_async_remote_copy(
            src_ref=send.at[block(d)], dst_ref=recv.at[block(me)],
            send_sem=send_sem.at[d], recv_sem=recv_sem.at[me],
            device_id=coords(d), device_id_type=MESH,
        )

    def fill(first):
        wanted = first * rows + lax.broadcasted_iota(jnp.int32, (n_owner * rows, shard), 0)
        pick = (wanted == place).astype(F32).astype(BF16)
        picked = jnp.dot(pick, unit[...], preferred_element_type=F32)
        lane_keys = keyrow[pl.ds(pl.multiple_of(first, 8), n_owner), 0:128]
        marks = jnp.broadcast_to(lane_keys[:, None, :], (n_owner, rows, 128)).reshape(n_owner * rows, 128)
        at_row = lax.broadcasted_iota(jnp.int32, (n_owner * rows, 128), 0) % rows
        head = jnp.where(at_row == cap, marks, picked[:, :128])
        where = pl.ds(pl.multiple_of(first * rows, rows), n_owner * rows)
        send[where, 0:128] = head.astype(BF16)
        send[where, 128:width] = picked[:, 128:].astype(BF16)

    fill(jnp.int32(devices))

    @pl.loop(0, n_owner)
    def _(i):
        o = lax.rem(my_owner + i, n_owner)
        target, copy = giant_copy(o)

        @pl.when(target != me)
        def _():
            copy.start()

        @pl.when(target == me)
        def _():
            giant[block(me), :] = send[block(devices + o), :]

    @pl.loop(0, n_split)
    def _(b):
        group = lax.rem(b + lax.div(me, n_owner), n_split)
        fill(group * n_owner)

        @pl.loop(0, n_owner)
        def _(i):
            d = group * n_owner + lax.rem(me + i, n_owner)

            @pl.when(d != me)
            def _():
                local_copy(d).start()

            @pl.when(d == me)
            def _():
                recv[block(me), :] = send[block(me), :]

    eye = lax.broadcasted_iota(jnp.int32, (rows, 128), 0) == lax.broadcasted_iota(jnp.int32, (rows, 128), 1)

    def group_best(buf, sem, send_first, to_group):
        best[...] = jnp.full_like(best, -1.0)

        def wait_source(q):
            @pl.when(q != me)
            def _():
                pltpu.make_async_remote_copy(
                    src_ref=send.at[block(0)], dst_ref=buf.at[block(q)],
                    send_sem=send_sem.at[0], recv_sem=sem.at[q],
                    device_id=coords(q), device_id_type=MESH,
                ).wait_recv()

        def pairs(ci, cj):
            ri = pl.ds(pl.multiple_of(ci * chunk, chunk), chunk)
            rj = pl.ds(pl.multiple_of(cj * chunk, chunk), chunk)
            scores = lax.dot_general(
                buf[ri, :], buf[rj, :], (((1,), (1,)), ((), ())), preferred_element_type=F32
            )
            ki = keycol[ri, 0:1]
            kj = keyrow[pl.ds(cj * 8, 1), 0:chunk]
            ii = lax.broadcasted_iota(jnp.int32, (chunk, chunk), 0) + (ci - cj) * chunk
            jj = lax.broadcasted_iota(jnp.int32, (chunk, chunk), 1)
            ok = (ki == kj) & (ii != jj)
            top = jnp.max(jnp.where(ok, scores, -1.0), axis=1, keepdims=True)
            best[ri, :] = jnp.maximum(best[ri, :], jnp.broadcast_to(top, (chunk, 128)))

        @pl.loop(0, chunks)
        def _(c):
            @pl.loop(0, per)
            def _(j):
                q = c * per + j
                wait_source(q)
                lane_keys = buf[block(q), 0:128].astype(F32)[cap:cap + 1, :]
                col = jnp.sum(jnp.where(eye, lane_keys, 0.0), axis=1, keepdims=True)
                keycol[block(q), :] = jnp.broadcast_to(col, (rows, 128))

            here = pl.ds(pl.multiple_of(c * chunk, chunk), chunk)
            cols = keycol[here, :]
            turned = jnp.transpose(cols)
            keyrow[pl.ds(pl.multiple_of(c * 8, 8), 8), 0:chunk] = jnp.where(turned[0:8, :] > 0.5, turned[0:8, :], -1.0)
            pairs(c, c)

            @pl.loop(0, c)
            def _(e):
                pairs(c, e)
                pairs(e, c)

        @pl.loop(0, devices)
        def _(i):
            q = lax.rem(me + i, devices)
            line = jnp.sum(jnp.where(eye, best[block(q), :], 0.0), axis=0, keepdims=True)
            resbuf[pl.ds(pl.multiple_of((send_first + q) * 8, 8), 1), :] = line

            @pl.when(q != me)
            def _():
                result_copy(send_first, q, to_group).start()

            @pl.when(q == me)
            def _():
                resrecv[pl.ds(pl.multiple_of(to_group * 8, 8), 8), :] = resbuf[
                    pl.ds(pl.multiple_of((send_first + q) * 8, 8), 8), :
                ]

    def result_copy(send_first, q, group):
        return pltpu.make_async_remote_copy(
            src_ref=resbuf.at[pl.ds(pl.multiple_of((send_first + q) * 8, 8), 8)],
            dst_ref=resrecv.at[pl.ds(pl.multiple_of(group * 8, 8), 8)],
            send_sem=res_send_sem.at[send_first + q], recv_sem=res_recv_sem.at[group],
            device_id=coords(q), device_id_type=MESH,
        )

    @pl.when(is_holder)
    def _():
        group_best(giant, giant_sem, devices, devices + my_owner)

    group_best(recv, recv_sem, 0, me)

    @pl.loop(0, n_owner)
    def _(o):
        target, copy = giant_copy(o)

        @pl.when(target != me)
        def _():
            copy.wait_send()

    @pl.loop(0, devices)
    def _(d):
        @pl.when(d != me)
        def _():
            local_copy(d).wait_send()
            result_copy(0, d, me).wait_send()

            @pl.when(is_holder)
            def _():
                result_copy(devices, d, devices + my_owner).wait_send()

    @pl.loop(0, ndest)
    def _(g):
        o = g - devices
        source = jnp.where(g < devices, g, o * n_split + holder_split(o))

        @pl.when(source != me)
        def _():
            result_copy(0, me, g).wait_recv()

    lines = jnp.concatenate([resrecv[g * 8:g * 8 + 1, :] for g in range(ndest)], axis=0)
    if gpad > ndest:
        lines = jnp.concatenate([lines, jnp.zeros((gpad - ndest, 128), F32)], axis=0)
    dest_again = dest_ref[...]
    hot = (lax.broadcasted_iota(jnp.int32, (gpad, shard), 0) == dest_again).astype(F32)
    found = lax.dot_general(
        lines, hot, (((0,), (0,)), ((), ())), preferred_element_type=F32, precision=lax.Precision.HIGHEST
    )
    out_ref[...] = jnp.sum(jnp.where(slot_hot > 0.5, found, 0.0), axis=0, keepdims=True)


def on_device(embeddings, row_dest, row_cluster):
    n_owner = lax.axis_size("owner")
    n_split = lax.axis_size("split")
    devices = n_owner * n_split
    ndest = devices + n_owner
    shard, width = embeddings.shape
    cap = max(2, 2 * shard // ndest)
    rows = (cap + 1 + 15) // 16 * 16
    per = 1
    while per * 2 <= devices and per * 2 * rows <= 512:
        per *= 2
    chunk = per * rows
    total = devices * rows
    keep = max((ndest + 15) // 16 * 16, devices // per * 8)
    vmem = pl.BlockSpec(memory_space=pltpu.VMEM)
    out = pl.pallas_call(
        functools.partial(kernel, (n_owner, n_split, cap, rows, per)),
        out_shape=jax.ShapeDtypeStruct((1, shard), F32),
        in_specs=[vmem] * 3,
        out_specs=vmem,
        scratch_shapes=[
            pltpu.VMEM((shard, width), BF16),
            pltpu.VMEM((ndest * rows, width), BF16),
            pltpu.VMEM((total, width), BF16),
            pltpu.VMEM((total, width), BF16),
            pltpu.VMEM((total, 128), F32),
            pltpu.VMEM((keep, max(128, chunk)), F32),
            pltpu.VMEM((total, 128), F32),
            pltpu.VMEM((2 * devices * 8, 128), F32),
            pltpu.VMEM((ndest * 8, 128), F32),
            pltpu.SemaphoreType.DMA((ndest,)),
            pltpu.SemaphoreType.DMA((devices,)),
            pltpu.SemaphoreType.DMA((devices,)),
            pltpu.SemaphoreType.DMA((2 * devices,)),
            pltpu.SemaphoreType.DMA((ndest,)),
        ],
        compiler_params=pltpu.CompilerParams(
            collective_id=0, has_side_effects=True, vmem_limit_bytes=56 * 1024 * 1024
        ),
    )(embeddings, row_dest.reshape(1, shard), row_cluster.reshape(1, shard))
    return out.reshape(shard)


def solution(mesh):
    placed = (P(("owner", "split"), None), P(("owner", "split"), None), P(("owner", "split")))
    return jax.shard_map(
        on_device, mesh=mesh, in_specs=placed, out_specs=P(("owner", "split")), check_vma=False
    )
```

time: 300 us -> 156 us (0.52)
  Pallas kernels: 0 us -> 154 us
  blocking collectives: 152 us -> 0 us
  local copies, waits for them, and re-layouts: 68.4 us -> 1.28 us
  starting transfers between devices: 22.1 us -> 0 us
  other arithmetic: 19.6 us -> 0 us
  between operations: 13.7 us -> 0.01 us
  waiting for transfers between devices: 11.2 us -> 0 us
  matrix products: 10.9 us -> 0 us
    pallas_call x0 -> x1, Pallas kernels: none -> 154 us  [on_device(): pl.pallas_call(functools.partial(kernel, (n_owner, n_split, cap, rows, pe...]
    all_gather x1 -> x0, blocking collectives: 140 us -> none  [on_device(): piece_keys = lax.all_gather(giant_keys, 'split', axis=0, tiled=True)]
    gather x5 -> x0, local copies, waits for them, and re-layouts: 36.2 us -> none  [the longest x2 16.1 us: on_device(): unit[safe_ids]]
    all_to_all x5 -> x0, starting transfers between devices: 22.1 us -> none  [the longest x1 6.32 us: on_device(): lax.all_to_all(local_keys, ('owner', 'split'), split_axis=0, concat_axis=...]
    all_to_all x1 -> x0, blocking collectives: 11.8 us -> none  [on_device(): lax.all_to_all(local_best, ('owner', 'split'), split_axis=0, concat_axis=...]
    another operation x3 -> x0, other arithmetic: 11.3 us -> none
    all_to_all x5 -> x0, waiting for transfers between devices: 11.1 us -> none  [the longest x1 9.71 us: on_device(): lax.all_to_all(send_rows[devices:], 'owner', split_axis=0, concat_axis=0,...]
    dot_general x3 -> x0, matrix products: 10.9 us -> none  [pair_scores(): lax.dot_general(left_rows, right_rows, (((1,), (1,)), ((), ())), preferre...]
  transfers between devices with their start and end apart: 6 -> 0, of which waited for: 2 -> 0; matrix products, arithmetic and copies ran while one was open for 18% -> 0% of each run, Pallas kernels for 0% -> 0%
where the time goes in v1:
time: 156 us; the launch traced here: 155 us
  Pallas kernels  154 us (99%)
    pallas_call x1, Pallas kernels, on_device(): pl.pallas_call(functools.partial(kernel, (n_owner, n_split, cap, rows, pe...  154 us

profile of v1, /device:TPU:0, one launch (start us, length us, event | category | flops | bytes accessed | tf_op | source)
XLA Modules:
  0.0 155.3 jit_solution(13832033994844255379)
XLA Ops:
  0.0 154.0 %shard_map.37 = f32[1,1024]{1,0:T(1,128)} custom-call(bf16[1024,1024]{1,0:T(8,128)(2,1)} %emb_ref.1, s32[1,1024]{1,0:T(1,128)} %bitcast.4, s32[1,1024]{1,0:T(1,128)} %bitcast.5), custom_call_target="tpu_custom_call" | custom-call | tf_op jit(solution)/shard_map/pallas_call | solution.py:268
  154.1 1.3 copy.5

commit v2 on v1

--- a/solution.py
+++ b/solution.py
@@ -14,14 +14,22 @@
 
 def kernel(
     sizes, emb_ref, dest_ref, cluster_ref, out_ref,
-    unit, send, recv, giant, keycol, keyrow, best, resbuf, resrecv,
-    send_sem, recv_sem, giant_sem, res_send_sem, res_recv_sem,
+    unit, send, recv, giant, keycol, keyrow, best, resbuf, resrecv, *rest
 ):
-    n_owner, n_split, cap, rows, per = sizes
+    n_owner, n_split, cap, rows, extra, per = sizes
+    send_sem, recv_sem, giant_sem, res_send_sem, res_recv_sem = rest[:5]
+    if extra:
+        send_x, recv_x, giant_x, send_x_sem, recv_x_sem, giant_x_sem = rest[5:]
+    else:
+        send_x = recv_x = giant_x = send_x_sem = recv_x_sem = giant_x_sem = None
     devices = n_owner * n_split
     ndest = devices + n_owner
     shard, width = emb_ref.shape
-    chunk = per * rows
+    pieces = width // 128
+    tall = extra * pieces
+    main = per * rows
+    chunk = per * (rows + extra)
+    pitch = rows + extra
     chunks = devices // per
     my_owner = lax.axis_index("owner")
     my_split = lax.axis_index("split")
@@ -37,6 +45,21 @@
 
     def block(number):
         return pl.ds(pl.multiple_of(number * rows, rows), rows)
+
+    def landing(q):
+        at = lax.div(q, per) * chunk + lax.rem(q, per) * rows
+        return pl.ds(pl.multiple_of(at, 16), rows)
+
+    def tail(number):
+        return pl.ds(pl.multiple_of(number * tall, tall), tall)
+
+    def place_of(index):
+        source, at = index // rows, index % rows
+        if extra:
+            after = index - main
+            source = jnp.where(after < 0, source, after // extra)
+            at = jnp.where(after < 0, at, rows + after % extra)
+        return source, at
 
     barrier = pltpu.get_barrier_semaphore()
 
@@ -61,7 +84,7 @@
     ).astype(F32).astype(BF16)
     before = jnp.dot(onehot.astype(BF16), earlier, preferred_element_type=F32)
     slot = jnp.sum(onehot * before, axis=0, keepdims=True).astype(jnp.int32)
-    place = dest * rows + slot
+    place = dest * pitch + slot
     key = jnp.where(dest < devices, cluster_ref[...], 0) + 1
     slot_hot = (lax.broadcasted_iota(jnp.int32, (128, shard), 0) == slot).astype(F32)
     keymat = lax.dot_general(
@@ -73,47 +96,77 @@
 
     pl.semaphore_wait(barrier, devices - 1)
 
-    def giant_copy(o):
+    def row_copies(src, dst, dst_x, sems, sems_x, number, target):
+        made = [
+            pltpu.make_async_remote_copy(
+                src_ref=send.at[block(number)], dst_ref=dst.at[landing(src)],
+                send_sem=send_sem.at[number], recv_sem=sems.at[src],
+                device_id=coords(target), device_id_type=MESH,
+            )
+        ]
+        if extra:
+            made.append(
+                pltpu.make_async_remote_copy(
+                    src_ref=send_x.at[tail(number)], dst_ref=dst_x.at[tail(src)],
+                    send_sem=send_x_sem.at[number], recv_sem=sems_x.at[src],
+                    device_id=coords(target), device_id_type=MESH,
+                )
+            )
+        return made
+
+    def giant_copies(o):
         target = o * n_split + holder_split(o)
-        return target, pltpu.make_async_remote_copy(
-            src_ref=send.at[block(devices + o)], dst_ref=giant.at[block(me)],
-            send_sem=send_sem.at[devices + o], recv_sem=giant_sem.at[me],
-            device_id=coords(target), device_id_type=MESH,
-        )
-
-    def local_copy(d):
-        return pltpu.make_async_remote_copy(
-            src_ref=send.at[block(d)], dst_ref=recv.at[block(me)],
-            send_sem=send_sem.at[d], recv_sem=recv_sem.at[me],
-            device_id=coords(d), device_id_type=MESH,
-        )
+        return target, row_copies(me, giant, giant_x, giant_sem, giant_x_sem, devices + o, target)
+
+    def local_copies(d):
+        return row_copies(me, recv, recv_x, recv_sem, recv_x_sem, d, d)
+
+    def keep_own(number, dst, dst_x):
+        dst[landing(me), :] = send[block(number), :]
+        if extra:
+            dst_x[tail(me), :] = send_x[tail(number), :]
+
+    def select(wanted):
+        pick = (wanted == place).astype(F32).astype(BF16)
+        return jnp.dot(pick, unit[...], preferred_element_type=F32)
 
     def fill(first):
-        wanted = first * rows + lax.broadcasted_iota(jnp.int32, (n_owner * rows, shard), 0)
-        pick = (wanted == place).astype(F32).astype(BF16)
-        picked = jnp.dot(pick, unit[...], preferred_element_type=F32)
         lane_keys = keyrow[pl.ds(pl.multiple_of(first, 8), n_owner), 0:128]
-        marks = jnp.broadcast_to(lane_keys[:, None, :], (n_owner, rows, 128)).reshape(n_owner * rows, 128)
-        at_row = lax.broadcasted_iota(jnp.int32, (n_owner * rows, 128), 0) % rows
-        head = jnp.where(at_row == cap, marks, picked[:, :128])
+        index = lax.broadcasted_iota(jnp.int32, (n_owner * rows, 1), 0)
+        picked = select((first + index // rows) * pitch + index % rows)
         where = pl.ds(pl.multiple_of(first * rows, rows), n_owner * rows)
-        send[where, 0:128] = head.astype(BF16)
-        send[where, 128:width] = picked[:, 128:].astype(BF16)
+        if extra:
+            send[where, :] = picked.astype(BF16)
+            index = lax.broadcasted_iota(jnp.int32, (n_owner * tall, 1), 0)
+            picked = select((first + index // tall) * pitch + rows + index % extra)
+            piece = index % tall // extra
+            laid = picked[:, 0:128]
+            for k in range(1, pieces):
+                laid = jnp.where(piece == k, picked[:, k * 128:(k + 1) * 128], laid)
+            marks = jnp.broadcast_to(lane_keys[:, None, :], (n_owner, tall, 128)).reshape(n_owner * tall, 128)
+            laid = jnp.where(index % tall == cap - rows, marks, laid)
+            send_x[pl.ds(pl.multiple_of(first * tall, tall), n_owner * tall), :] = laid.astype(BF16)
+        else:
+            marks = jnp.broadcast_to(lane_keys[:, None, :], (n_owner, rows, 128)).reshape(n_owner * rows, 128)
+            head = jnp.where(index % rows == cap, marks, picked[:, :128])
+            send[where, 0:128] = head.astype(BF16)
+            send[where, 128:width] = picked[:, 128:].astype(BF16)
 
     fill(jnp.int32(devices))
 
     @pl.loop(0, n_owner)
     def _(i):
         o = lax.rem(my_owner + i, n_owner)
-        target, copy = giant_copy(o)
+        target, copies = giant_copies(o)
 
         @pl.when(target != me)
         def _():
-            copy.start()
+            for copy in copies:
+                copy.start()
 
         @pl.when(target == me)
         def _():
-            giant[block(me), :] = send[block(devices + o), :]
+            keep_own(devices + o, giant, giant_x)
 
     @pl.loop(0, n_split)
     def _(b):
@@ -126,29 +179,39 @@
 
             @pl.when(d != me)
             def _():
-                local_copy(d).start()
+                for copy in local_copies(d):
+                    copy.start()
 
             @pl.when(d == me)
             def _():
-                recv[block(me), :] = send[block(me), :]
-
-    eye = lax.broadcasted_iota(jnp.int32, (rows, 128), 0) == lax.broadcasted_iota(jnp.int32, (rows, 128), 1)
-
-    def group_best(buf, sem, send_first, to_group):
+                keep_own(me, recv, recv_x)
+
+    row_source, row_slot = place_of(lax.broadcasted_iota(jnp.int32, (chunk, 1), 0))
+    lane_source, _ = place_of(lax.broadcasted_iota(jnp.int32, (1, chunk), 1))
+    at_slot = lax.broadcasted_iota(jnp.int32, (chunk, 128), 1) == row_slot
+    from_source = (lax.broadcasted_iota(jnp.int32, (max(per, 8), chunk), 0) == lane_source).astype(F32)
+    key_rows = per * (tall if extra else rows)
+    key_step, key_at = (tall, cap - rows) if extra else (rows, cap)
+    key_pick = (
+        lax.broadcasted_iota(jnp.int32, (chunk, key_rows), 1) == row_source * key_step + key_at
+    ).astype(F32).astype(BF16)
+    if extra:
+        low = lax.broadcasted_iota(jnp.int32, (per * extra, per * tall), 0)
+        high = lax.broadcasted_iota(jnp.int32, (per * extra, per * tall), 1)
+        low = low // extra * tall + low % extra
+
+    def group_best(buf, buf_x, sem, sem_x, send_first, to_group):
         best[...] = jnp.full_like(best, -1.0)
 
         def wait_source(q):
             @pl.when(q != me)
             def _():
-                pltpu.make_async_remote_copy(
-                    src_ref=send.at[block(0)], dst_ref=buf.at[block(q)],
-                    send_sem=send_sem.at[0], recv_sem=sem.at[q],
-                    device_id=coords(q), device_id_type=MESH,
-                ).wait_recv()
+                for copy in row_copies(q, buf, buf_x, sem, sem_x, 0, q):
+                    copy.wait_recv()
 
         def pairs(ci, cj):
-            ri = pl.ds(pl.multiple_of(ci * chunk, chunk), chunk)
-            rj = pl.ds(pl.multiple_of(cj * chunk, chunk), chunk)
+            ri = pl.ds(pl.multiple_of(ci * chunk, 16), chunk)
+            rj = pl.ds(pl.multiple_of(cj * chunk, 16), chunk)
             scores = lax.dot_general(
                 buf[ri, :], buf[rj, :], (((1,), (1,)), ((), ())), preferred_element_type=F32
             )
@@ -164,14 +227,22 @@
         def _(c):
             @pl.loop(0, per)
             def _(j):
-                q = c * per + j
-                wait_source(q)
-                lane_keys = buf[block(q), 0:128].astype(F32)[cap:cap + 1, :]
-                col = jnp.sum(jnp.where(eye, lane_keys, 0.0), axis=1, keepdims=True)
-                keycol[block(q), :] = jnp.broadcast_to(col, (rows, 128))
-
-            here = pl.ds(pl.multiple_of(c * chunk, chunk), chunk)
-            cols = keycol[here, :]
+                wait_source(c * per + j)
+
+            here = pl.ds(pl.multiple_of(c * chunk, 16), chunk)
+            if extra:
+                tiles = buf_x[pl.ds(pl.multiple_of(c * key_rows, key_rows), key_rows), :]
+                for k in range(pieces):
+                    gather = (high == low + k * extra).astype(F32).astype(BF16)
+                    buf[pl.ds(pl.multiple_of(c * chunk + main, 16), per * extra), k * 128:(k + 1) * 128] = jnp.dot(
+                        gather, tiles, preferred_element_type=F32
+                    ).astype(BF16)
+            else:
+                tiles = buf[here, 0:128]
+            lane_keys = jnp.dot(key_pick, tiles, preferred_element_type=F32)
+            col = jnp.sum(jnp.where(at_slot, lane_keys, 0.0), axis=1, keepdims=True)
+            cols = jnp.broadcast_to(col, (chunk, 128))
+            keycol[here, :] = cols
             turned = jnp.transpose(cols)
             keyrow[pl.ds(pl.multiple_of(c * 8, 8), 8), 0:chunk] = jnp.where(turned[0:8, :] > 0.5, turned[0:8, :], -1.0)
             pairs(c, c)
@@ -181,21 +252,29 @@
                 pairs(c, e)
                 pairs(e, c)
 
-        @pl.loop(0, devices)
-        def _(i):
-            q = lax.rem(me + i, devices)
-            line = jnp.sum(jnp.where(eye, best[block(q), :], 0.0), axis=0, keepdims=True)
-            resbuf[pl.ds(pl.multiple_of((send_first + q) * 8, 8), 1), :] = line
-
-            @pl.when(q != me)
-            def _():
-                result_copy(send_first, q, to_group).start()
-
-            @pl.when(q == me)
-            def _():
-                resrecv[pl.ds(pl.multiple_of(to_group * 8, 8), 8), :] = resbuf[
-                    pl.ds(pl.multiple_of((send_first + q) * 8, 8), 8), :
-                ]
+        @pl.loop(0, chunks)
+        def _(c):
+            here = pl.ds(pl.multiple_of(c * chunk, 16), chunk)
+            lines = jnp.dot(
+                from_source, jnp.where(at_slot, best[here, :], 0.0),
+                preferred_element_type=F32, precision=lax.Precision.HIGHEST,
+            )
+            for j in range(per):
+                resbuf[pl.ds(pl.multiple_of((send_first + c * per + j) * 8, 8), 1), :] = lines[j:j + 1, :]
+
+            @pl.loop(0, per)
+            def _(j):
+                q = c * per + j
+
+                @pl.when(q != me)
+                def _():
+                    result_copy(send_first, q, to_group).start()
+
+                @pl.when(q == me)
+                def _():
+                    resrecv[pl.ds(pl.multiple_of(to_group * 8, 8), 8), :] = resbuf[
+                        pl.ds(pl.multiple_of((send_first + q) * 8, 8), 8), :
+                    ]
 
     def result_copy(send_first, q, group):
         return pltpu.make_async_remote_copy(
@@ -207,23 +286,25 @@
 
     @pl.when(is_holder)
     def _():
-        group_best(giant, giant_sem, devices, devices + my_owner)
-
-    group_best(recv, recv_sem, 0, me)
+        group_best(giant, giant_x, giant_sem, giant_x_sem, devices, devices + my_owner)
+
+    group_best(recv, recv_x, recv_sem, recv_x_sem, 0, me)
 
     @pl.loop(0, n_owner)
     def _(o):
-        target, copy = giant_copy(o)
+        target, copies = giant_copies(o)
 
         @pl.when(target != me)
         def _():
-            copy.wait_send()
+            for copy in copies:
+                copy.wait_send()
 
     @pl.loop(0, devices)
     def _(d):
         @pl.when(d != me)
         def _():
-            local_copy(d).wait_send()
+            for copy in local_copies(d):
+                copy.wait_send()
             result_copy(0, d, me).wait_send()
 
             @pl.when(is_holder)
@@ -257,16 +338,30 @@
     ndest = devices + n_owner
     shard, width = embeddings.shape
     cap = max(2, 2 * shard // ndest)
-    rows = (cap + 1 + 15) // 16 * 16
+    rows, extra = cap // 16 * 16, cap + 1 - cap // 16 * 16
+    extra += extra % 2
+    if rows == 0 or extra > 8 or extra * (width // 128) % 16:
+        rows, extra = (cap + 1 + 15) // 16 * 16, 0
+    tall = extra * (width // 128)
     per = 1
-    while per * 2 <= devices and per * 2 * rows <= 512:
+    while per * 2 <= devices and per * 2 * (rows + extra) <= 512:
         per *= 2
-    chunk = per * rows
-    total = devices * rows
+    chunk = per * (rows + extra)
+    total = devices * (rows + extra)
     keep = max((ndest + 15) // 16 * 16, devices // per * 8)
     vmem = pl.BlockSpec(memory_space=pltpu.VMEM)
+    tails = []
+    if extra:
+        tails = [
+            pltpu.VMEM((ndest * tall, 128), BF16),
+            pltpu.VMEM((devices * tall, 128), BF16),
+            pltpu.VMEM((devices * tall, 128), BF16),
+            pltpu.SemaphoreType.DMA((ndest,)),
+            pltpu.SemaphoreType.DMA((devices,)),
+            pltpu.SemaphoreType.DMA((devices,)),
+        ]
     out = pl.pallas_call(
-        functools.partial(kernel, (n_owner, n_split, cap, rows, per)),
+        functools.partial(kernel, (n_owner, n_split, cap, rows, extra, per)),
         out_shape=jax.ShapeDtypeStruct((1, shard), F32),
         in_specs=[vmem] * 3,
         out_specs=vmem,
@@ -285,7 +380,7 @@
             pltpu.SemaphoreType.DMA((devices,)),
             pltpu.SemaphoreType.DMA((2 * devices,)),
             pltpu.SemaphoreType.DMA((ndest,)),
-        ],
+        ] + tails,
         compiler_params=pltpu.CompilerParams(
             collective_id=0, has_side_effects=True, vmem_limit_bytes=56 * 1024 * 1024
         ),

time: 156 us -> 130 us (0.83)
  Pallas kernels: 154 us -> 128 us
    pallas_call x1, Pallas kernels: 154 us -> 128 us  [on_device(): pl.pallas_call(functools.partial(kernel, (n_owner, n_split, cap, rows, ex...]
where the time goes in v2:
time: 130 us
  Pallas kernels  128 us (98%)
    pallas_call x1, Pallas kernels, on_device(): pl.pallas_call(functools.partial(kernel, (n_owner, n_split, cap, rows, ex...  128 us

profile of v2, /device:TPU:0, one launch (start us, length us, event | category | flops | bytes accessed | tf_op | source)
XLA Modules:
  0.0 129.5 jit_solution(16899603918799963701)
XLA Ops:
  0.0 128.2 %shard_map.37 = f32[1,1024]{1,0:T(1,128)} custom-call(bf16[1024,1024]{1,0:T(8,128)(2,1)} %emb_ref.1, s32[1,1024]{1,0:T(1,128)} %bitcast.4, s32[1,1024]{1,0:T(1,128)} %bitcast.5), custom_call_target="tpu_custom_call" | custom-call | tf_op jit(solution)/shard_map/pallas_call | solution.py:363
  128.3 1.3 copy.5

commit v3 on v2

--- a/solution.py
+++ b/solution.py
@@ -33,7 +33,14 @@
     chunks = devices // per
     my_owner = lax.axis_index("owner")
     my_split = lax.axis_index("split")
-    me = my_owner * n_split + my_split
+    me = my_split * n_owner + my_owner
+
+    def walk(start, step, count):
+        if count % 2:
+            return lax.rem(start + step, count)
+        half = count // 2
+        side = lax.rem(lax.div(start, half) + lax.div(step, half), 2)
+        return side * half + lax.rem(lax.rem(start, half) + lax.rem(step, half), half)
 
     def holder_split(o):
         return n_split // 2 - 1 + lax.rem(o, 2)
@@ -41,7 +48,7 @@
     is_holder = my_split == holder_split(my_owner)
 
     def coords(d):
-        return (lax.div(d, n_split), lax.rem(d, n_split))
+        return (lax.rem(d, n_owner), lax.div(d, n_owner))
 
     def block(number):
         return pl.ds(pl.multiple_of(number * rows, rows), rows)
@@ -76,13 +83,24 @@
         scale = lax.rsqrt(jnp.sum(values * values, axis=1, keepdims=True) + 1e-06)
         unit[at, :] = (values * scale).astype(BF16)
 
-    dest = dest_ref[...]
+    def renumbered():
+        named = dest_ref[...]
+        return jnp.where(named < devices, named % n_split * n_owner + named // n_split, named)
+
+    dest = renumbered()
     gpad = (ndest + 15) // 16 * 16
     onehot = (lax.broadcasted_iota(jnp.int32, (gpad, shard), 0) == dest).astype(F32)
+    span = 128
     earlier = (
-        lax.broadcasted_iota(jnp.int32, (shard, shard), 0) < lax.broadcasted_iota(jnp.int32, (shard, shard), 1)
+        lax.broadcasted_iota(jnp.int32, (span, span), 0) < lax.broadcasted_iota(jnp.int32, (span, span), 1)
     ).astype(F32).astype(BF16)
-    before = jnp.dot(onehot.astype(BF16), earlier, preferred_element_type=F32)
+    seen = jnp.zeros((gpad, 1), F32)
+    counts = []
+    for k in range(0, shard, span):
+        part = onehot[:, k:k + span]
+        counts.append(seen + jnp.dot(part.astype(BF16), earlier, preferred_element_type=F32))
+        seen = seen + jnp.sum(part, axis=1, keepdims=True)
+    before = jnp.concatenate(counts, axis=1)
     slot = jnp.sum(onehot * before, axis=0, keepdims=True).astype(jnp.int32)
     place = dest * pitch + slot
     key = jnp.where(dest < devices, cluster_ref[...], 0) + 1
@@ -115,7 +133,7 @@
         return made
 
     def giant_copies(o):
-        target = o * n_split + holder_split(o)
+        target = holder_split(o) * n_owner + o
         return target, row_copies(me, giant, giant_x, giant_sem, giant_x_sem, devices + o, target)
 
     def local_copies(d):
@@ -170,7 +188,7 @@
 
     @pl.loop(0, n_split)
     def _(b):
-        group = lax.rem(b + lax.div(me, n_owner), n_split)
+        group = walk(my_split, b, n_split)
         fill(group * n_owner)
 
         @pl.loop(0, n_owner)
@@ -223,8 +241,12 @@
             top = jnp.max(jnp.where(ok, scores, -1.0), axis=1, keepdims=True)
             best[ri, :] = jnp.maximum(best[ri, :], jnp.broadcast_to(top, (chunk, 128)))
 
+        my_chunk = lax.div(me, per)
+
         @pl.loop(0, chunks)
-        def _(c):
+        def _(step):
+            c = walk(my_chunk, step, chunks)
+
             @pl.loop(0, per)
             def _(j):
                 wait_source(c * per + j)
@@ -247,8 +269,9 @@
             keyrow[pl.ds(pl.multiple_of(c * 8, 8), 8), 0:chunk] = jnp.where(turned[0:8, :] > 0.5, turned[0:8, :], -1.0)
             pairs(c, c)
 
-            @pl.loop(0, c)
-            def _(e):
+            @pl.loop(0, step)
+            def _(done):
+                e = walk(my_chunk, done, chunks)
                 pairs(c, e)
                 pairs(e, c)
 
@@ -314,7 +337,7 @@
     @pl.loop(0, ndest)
     def _(g):
         o = g - devices
-        source = jnp.where(g < devices, g, o * n_split + holder_split(o))
+        source = jnp.where(g < devices, g, holder_split(o) * n_owner + o)
 
         @pl.when(source != me)
         def _():
@@ -323,7 +346,7 @@
     lines = jnp.concatenate([resrecv[g * 8:g * 8 + 1, :] for g in range(ndest)], axis=0)
     if gpad > ndest:
         lines = jnp.concatenate([lines, jnp.zeros((gpad - ndest, 128), F32)], axis=0)
-    dest_again = dest_ref[...]
+    dest_again = renumbered()
     hot = (lax.broadcasted_iota(jnp.int32, (gpad, shard), 0) == dest_again).astype(F32)
     found = lax.dot_general(
         lines, hot, (((0,), (0,)), ((), ())), preferred_element_type=F32, precision=lax.Precision.HIGHEST

time: 130 us -> 123 us (0.946)
  Pallas kernels: 128 us -> 122 us
    pallas_call x1, Pallas kernels: 128 us -> 122 us  [on_device(): pl.pallas_call(functools.partial(kernel, (n_owner, n_split, cap, rows, ex...]
where the time goes in v3:
time: 123 us
  Pallas kernels  122 us (99%)
  local copies, waits for them, and re-layouts  1.28 us (1%)
    pallas_call x1, Pallas kernels, on_device(): pl.pallas_call(functools.partial(kernel, (n_owner, n_split, cap, rows, ex...  122 us

profile of v3, /device:TPU:0, one launch (start us, length us, event | category | flops | bytes accessed | tf_op | source)
XLA Modules:
  0.0 122.8 jit_solution(14192640869334317651)
XLA Ops:
  0.0 121.5 %shard_map.37 = f32[1,1024]{1,0:T(1,128)} custom-call(bf16[1024,1024]{1,0:T(8,128)(2,1)} %emb_ref.1, s32[1,1024]{1,0:T(1,128)} %bitcast.4, s32[1,1024]{1,0:T(1,128)} %bitcast.5), custom_call_target="tpu_custom_call" | custom-call | tf_op jit(solution)/shard_map/pallas_call | solution.py:386
  121.5 1.3 %copy.5 = f32[1024]{0:T(1024)} copy(f32[1024]{0:T(1024)} %bitcast.3) | data formatting | bytes 8192

commit v4 on v3

--- a/solution.py
+++ b/solution.py
@@ -227,7 +227,7 @@
                 for copy in row_copies(q, buf, buf_x, sem, sem_x, 0, q):
                     copy.wait_recv()
 
-        def pairs(ci, cj):
+        def pairs(ci, cj, both):
             ri = pl.ds(pl.multiple_of(ci * chunk, 16), chunk)
             rj = pl.ds(pl.multiple_of(cj * chunk, 16), chunk)
             scores = lax.dot_general(
@@ -238,8 +238,12 @@
             ii = lax.broadcasted_iota(jnp.int32, (chunk, chunk), 0) + (ci - cj) * chunk
             jj = lax.broadcasted_iota(jnp.int32, (chunk, chunk), 1)
             ok = (ki == kj) & (ii != jj)
-            top = jnp.max(jnp.where(ok, scores, -1.0), axis=1, keepdims=True)
+            kept = jnp.where(ok, scores, -1.0)
+            top = jnp.max(kept, axis=1, keepdims=True)
             best[ri, :] = jnp.maximum(best[ri, :], jnp.broadcast_to(top, (chunk, 128)))
+            if both:
+                down = jnp.broadcast_to(jnp.max(kept, axis=0, keepdims=True), (128, chunk))
+                best[rj, :] = jnp.maximum(best[rj, :], jnp.transpose(down))
 
         my_chunk = lax.div(me, per)
 
@@ -267,13 +271,12 @@
             keycol[here, :] = cols
             turned = jnp.transpose(cols)
             keyrow[pl.ds(pl.multiple_of(c * 8, 8), 8), 0:chunk] = jnp.where(turned[0:8, :] > 0.5, turned[0:8, :], -1.0)
-            pairs(c, c)
+            pairs(c, c, False)
 
             @pl.loop(0, step)
             def _(done):
                 e = walk(my_chunk, done, chunks)
-                pairs(c, e)
-                pairs(e, c)
+                pairs(c, e, True)
 
         @pl.loop(0, chunks)
         def _(c):

time: 123 us -> 122 us (level)
  Pallas kernels: 122 us -> 120 us
where the time goes in v4:
time: 122 us
  Pallas kernels  120 us (98%)
  local copies, waits for them, and re-layouts  1.28 us (1%)
    pallas_call x1, Pallas kernels, on_device(): pl.pallas_call(functools.partial(kernel, (n_owner, n_split, cap, rows, ex...  120 us

profile of v4, /device:TPU:0, one launch (start us, length us, event | category | flops | bytes accessed | tf_op | source)
XLA Modules:
  0.0 121.6 jit_solution(15623020372392894562)
XLA Ops:
  0.0 120.3 %shard_map.37 = f32[1,1024]{1,0:T(1,128)} custom-call(bf16[1024,1024]{1,0:T(8,128)(2,1)} %emb_ref.1, s32[1,1024]{1,0:T(1,128)} %bitcast.4, s32[1,1024]{1,0:T(1,128)} %bitcast.5), custom_call_target="tpu_custom_call" | custom-call | tf_op jit(solution)/shard_map/pallas_call | solution.py:389
  120.3 1.3 %copy.5 = f32[1024]{0:T(1024)} copy(f32[1024]{0:T(1024)} %bitcast.3) | data formatting | bytes 8192
